TPU v7x, 32 devices: a whole 2x2x4 slice. The times are simulated.
32 devices in a mesh: run: 2 (over y), tile: 4 (over z), site: 2 (over x), freq: 2 (over core).
Axes of the slice: x: 2, y: 2, z: 4, core: 2. Of those that a mesh axis runs over, the one named last changes fastest.
Arguments:
- jacobian: bfloat16 [256, 16, 8, 8, 128], P(('run', 'tile', 'site'), None, 'freq'), parts along dimension 0, may hold values from -6 to 6
- footprint: int32 [256, 16], P(('run', 'tile', 'site')), parts along dimension 0, may hold values from 0 to 4095, as said below
- home: int32 [8192], P('run'), parts along dimension 0, may hold values from 0 to 4095, as said below
- residual: float32 [256, 8, 8], P(('run', 'tile', 'site'), 'freq'), parts along dimension 0, may hold values from -6 to 6
- weights: float32 [256], P(('run', 'tile', 'site')), parts along dimension 0, may hold values from 0.2 to 2
- damping: float32 [8192, 128], P(('run', 'tile', 'site')), parts along dimension 0, may hold values from 2 to 50
- step_lengths: float32 [8], replicated, may hold values from 0.2 to 1.2
Outputs:
- model_step: float32 [8192, 128], P(('run', 'tile', 'site')), parts along dimension 0
- change: float32 [256, 8, 8], P(('run', 'tile', 'site'), 'freq'), parts along dimension 0
- curve: float32 [16, 8], P(('run', 'freq')), parts along dimension 0
There are 2 independent parts, one for each index of `run`. A program takes and returns all parts, laid end to end along the dimension named above; an argument that names none is the same for every part. Nothing has to cross between parts.
Inputs may be any that keep to these rules, and one draw needn't show every extreme that they name: home is a permutation of 0 to 4095. `footprint`: of the 256 entries of each aligned block of 16 sites, at most 64 have home[block] // 512 equal to any one value; one value receives exactly 64 entries from every such block.
All inputs are finite; a program needn't handle non-finite values.
Results may differ from a plain program's by a relative error of at most 0.0029.
Values may be sent and summed in bfloat16 or wider, within the bound.
A program may use at most 64 MiB of HBM per device.

v0:
```python
import jax
import jax.numpy as jnp
from jax import lax
from jax.sharding import PartitionSpec as P


def shards(jacobian, footprint, home, residual, weights, damping, step_lengths):
    site_count, foot_count, freq_local, comps, width = jacobian.shape
    blocks_dev = damping.shape[0]
    tiles = lax.axis_size("tile")
    groups = lax.axis_size("site")
    owner_count = tiles * groups
    entries = site_count * foot_count
    capacity = 2 * entries // owner_count
    weighted = (weights[:, None, None] * residual).astype(jnp.bfloat16)
    grad_terms = jnp.einsum(
        "skfcb,sfc->skb", jacobian, weighted, preferred_element_type=jnp.float32
    )
    curve_terms = weights[:, None, None] * jnp.sum(
        jnp.square(jacobian.astype(jnp.float32)), axis=(2, 3)
    )
    terms = jnp.concatenate([grad_terms, curve_terms], axis=-1).reshape(entries, 2 * width)
    position = home[footprint.reshape(-1)]
    dest_rank = position // blocks_dev
    local_slot = position % blocks_dev
    member = (dest_rank[:, None] == jnp.arange(owner_count, dtype=jnp.int32)[None, :]).astype(
        jnp.int32
    )
    earlier = jnp.cumsum(member, axis=0) - member
    order_in = jnp.sum(earlier * member, axis=1)
    bucket = dest_rank * capacity + order_in
    outgoing = jnp.zeros((owner_count * capacity, 2 * width), jnp.float32).at[bucket].set(terms)
    out_slots = (
        jnp.full((owner_count * capacity,), blocks_dev, jnp.int32).at[bucket].set(local_slot)
    )
    received, in_slots = (
        lax.all_to_all(
            outgoing.reshape(owner_count, capacity, 2 * width),
            ("tile", "site"),
            split_axis=0,
            concat_axis=0,
            tiled=True,
        ),
        lax.all_to_all(
            out_slots.reshape(owner_count, capacity),
            ("tile", "site"),
            split_axis=0,
            concat_axis=0,
            tiled=True,
        ),
    )
    flat_slots = in_slots.reshape(-1)
    totals = jax.ops.segment_sum(
        received.reshape(-1, 2 * width), flat_slots, num_segments=blocks_dev + 1
    )[:blocks_dev]
    totals = lax.psum(totals, "freq")
    model_step = totals[:, :width] / (totals[:, width:] + damping)
    step_low = jnp.concatenate(
        [model_step.astype(jnp.bfloat16), jnp.zeros((1, width), jnp.bfloat16)], axis=0
    )
    reply = step_low[flat_slots]
    returned = lax.all_to_all(
        reply.reshape(owner_count, capacity, width),
        ("tile", "site"),
        split_axis=0,
        concat_axis=0,
        tiled=True,
    )
    entry_rows = returned.reshape(owner_count * capacity, width)[bucket]
    entry_step = entry_rows.reshape(site_count, foot_count, width)
    change = jnp.einsum("skfcb,skb->sfc", jacobian, entry_step, preferred_element_type=jnp.float32)
    scale_total = site_count * owner_count * comps
    gap = residual[:, :, :, None] - step_lengths[None, None, None, :] * change[:, :, :, None]
    partial_sum = jnp.einsum("s,sfca->fa", weights, gap * gap)
    curve = lax.psum(partial_sum, ("tile", "site")) / scale_total
    return (model_step, change, curve)


def solution(mesh):
    placed = (
        P(("run", "tile", "site"), None, "freq", None, None),
        P(("run", "tile", "site"), None),
        P("run"),
        P(("run", "tile", "site"), "freq", None),
        P(("run", "tile", "site")),
        P(("run", "tile", "site"), None),
        P(),
    )
    return jax.shard_map(
        shards,
        mesh=mesh,
        in_specs=placed,
        out_specs=(
            P(("run", "tile", "site"), None),
            P(("run", "tile", "site"), "freq", None),
            P(("run", "freq"), None),
        ),
        check_vma=False,
    )
```

profile of v0, /device:TPU:0, one launch (start us, length us, event | category | flops | bytes accessed | tf_op | source)
XLA Modules:
  0.0 117.0 jit_solution(13052791357690887810)
XLA Ops:
  7.2 0.0 copy-start
  7.2 0.0 copy-start.1
  7.2 0.0 copy-start.5
  7.2 0.0 copy-start.4
  7.2 0.9 reshape.181
  8.2 0.0 copy-done
  8.2 1.7 %gather_fusion = s32[256]{0:T(256)S(1)} fusion(s32[4096]{0:T(1024)S(1)} %copy-done, s32[1024]{0:T(1024)S(1)} %pad_clamp_fusion.2), kind=kCustom, calls=%fused_computation | custom fusion | bytes 3072 | tf_op jit(solution)/shard_map/gather | solution.py:23
  9.9 0.6 reduce-window.6
  10.5 0.2 slice_reduce_fusion
  10.8 0.1 fusion.10
  10.9 1.4 %scatter_custom_fusion = s32[512]{0:T(512)S(1)} fusion(s32[256]{0:T(256)S(1)} %bitcast.64, s32[256]{0:T(256)S(1)} %get-tuple-element.5, s32[]{:T(128)} %constant.41.clone.1), kind=kCustom, calls=%fused_computation.49 | custom fusion | bytes 2052 | tf_op jit(solution)/shard_map/scatter | solution.py:34
  12.3 0.7 all_to_all.12
  13.0 7.3 %all-to-all-start = ((s32[8,1,64]{2,1,0:T(1,128)}), s32[8,1,64]{2,1,0:T(1,128)S(1)}, u32[]{:S(2)}, u32[]{:S(2)}) async-start(s32[8,1,64]{2,1,0:T(1,128)} %all_to_all.12), calls=%async_computation | async-start | bytes 8192 | tf_op jit(solution)/shard_map/all_to_all | solution.py:44
  20.2 2.3 %multiply_reduce_fusion = f32[16,16,128]{2,1,0:T(8,128)S(1)} fusion(bf16[16,16,4,8,128]{4,3,2,1,0:T(8,128)(2,1)} %param.7), kind=kLoop, calls=%fused_computation.6 | loop fusion | flops 3112960 | bytes 2228224 | tf_op jit(solution)/shard_map/reduce_sum | solution.py:19
  22.6 0.0 copy-done.5
  22.6 0.1 broadcast_multiply_fusion
  22.7 0.0 copy-done.4
  22.7 0.1 copy.14
  22.8 0.0 copy-done.1
  22.8 0.6 fusion.22
  23.4 0.0 copy-start.2
  23.4 2.2 %scatter_custom_fusion.1 = f32[512,256]{1,0:T(8,128)} fusion(s32[256]{0:T(256)S(1)} %bitcast.65, f32[256,256]{1,0:T(8,128)S(1)} %bitcast.56, f32[]{:T(128)} %constant.40.clone.1), kind=kCustom, calls=%fused_computation.14 | custom fusion | bytes 524292 | tf_op jit(solution)/shard_map/scatter | solution.py:32
  25.6 1.0 all-to-all-done
  26.6 5.0 %all-to-all-start.1 = ((f32[8,64,256]{2,1,0:T(8,128)}), f32[8,64,256]{2,1,0:T(8,128)S(1)}, u32[]{:S(2)}, u32[]{:S(2)}) async-start(f32[8,64,256]{2,1,0:T(8,128)} %bitcast.11), calls=%async_computation.1 | async-start | bytes 1048576 | tf_op jit(solution)/shard_map/all_to_all | solution.py:37
  31.6 0.0 all-reduce.3.cloned.1.call-start
  31.7 0.5 broadcast.204
  32.2 0.7 reduce.7
  32.8 0.1 reshape.231
  32.9 12.7 %all-to-all-done.1 = f32[8,64,256]{2,1,0:T(8,128)S(1)} async-done(((f32[8,64,256]{2,1,0:T(8,128)}), f32[8,64,256]{2,1,0:T(8,128)S(1)}, u32[]{:S(2)}, u32[]{:S(2)}) %all-to-all-start.1) | async-done | bytes 524320 | tf_op jit(solution)/shard_map/all_to_all | solution.py:37
  45.6 3.7 %scatter_custom_fusion.2 = f32[513,256]{1,0:T(8,128)S(1)} fusion(s32[512]{0:T(512)S(1)} %reshape.231, f32[512,256]{1,0:T(8,128)S(1)} %bitcast.54, f32[]{:T(128)} %constant.40.clone.1), kind=kCustom, calls=%fused_computation.9 | custom fusion | flops 131072 | bytes 525316 | tf_op jit(solution)/shard_map/scatter-add | solution.py:53
  49.3 0.8 slice.27
  50.1 0.0 all-reduce.3.cloned.1.call-update
  50.1 0.1 broadcast_in_dim_reshape.3
  50.2 17.9 %all-reduce.3.cloned.1.call-done = f32[512,256]{1,0:T(8,128)} async-done(((f32[512,256]{1,0:T(8,128)}), f32[512,256]{1,0:T(8,128)}) %all-reduce.3.cloned.1.call-update) | async-done | bytes 524304 | tf_op jit(solution)/shard_map/psum | solution.py:56
  68.1 0.0 copy-done.2
  68.1 1.8 %fusion.17 = (bf16[512,128]{1,0:T(8,128)(2,1)S(1)}, f32[512,128]{1,0:T(8,128)}) fusion(f32[512,128]{1,0:T(8,128)S(1)} %copy-done.2, f32[512,256]{1,0:T(8,128)} %all-reduce.3.cloned.1.call-done), kind=kLoop, calls=%fused_computation.55 | loop fusion | flops 196608 | bytes 1179648 | tf_op jit(solution)/shard_map/convert_element_type | solution.py:59
  69.9 1.9 %gather_fusion.1 = bf16[512,128]{1,0:T(8,128)(2,1)} fusion(bf16[513,128]{1,0:T(8,128)(2,1)S(1)} %concatenate.7, s32[1024]{0:T(1024)S(1)} %pad_clamp_fusion.1), kind=kCustom, calls=%fused_computation.1 | custom fusion | bytes 264192 | tf_op jit(solution)/shard_map/gather | solution.py:61
  71.8 5.8 %all-to-all-start.2 = ((bf16[8,64,128]{2,1,0:T(8,128)(2,1)}), bf16[8,64,128]{2,1,0:T(8,128)(2,1)S(1)}, u32[]{:S(2)}, u32[]{:S(2)}) async-start(bf16[8,64,128]{2,1,0:T(8,128)(2,1)} %bitcast.14), calls=%async_computation.2 | async-start | bytes 262144 | tf_op jit(solution)/shard_map/all_to_all | solution.py:62
  77.6 7.4 %all-to-all-done.2 = bf16[8,64,128]{2,1,0:T(8,128)(2,1)S(1)} async-done(((bf16[8,64,128]{2,1,0:T(8,128)(2,1)}), bf16[8,64,128]{2,1,0:T(8,128)(2,1)S(1)}, u32[]{:S(2)}, u32[]{:S(2)}) %all-to-all-start.2) | async-done | bytes 131104 | tf_op jit(solution)/shard_map/all_to_all | solution.py:62
  85.1 0.0 copy-start.6
  85.1 0.9 gather_fusion.2
  85.9 4.7 %fusion = f32[16,1,4,8,1]{3,1,4,2,0:T(1,128)S(1)} fusion(bf16[16,16,4,8,128]{4,3,2,1,0:T(8,128)(2,1)S(1)} %copy-done.1, bf16[16,16,128,1,1]{2,1,0,3,4:T(8,128)(2,1)S(1)} %bitcast.57), kind=kOutput, calls=%fused_computation.7 | convolution fusion | flops 2097152 | bytes 2164736 | tf_op jit(solution)/shard_map/skfcb,skb->sfc/dot_general | solution.py:71
  90.6 0.1 copy.18
  90.7 0.0 copy-start.3
  90.7 0.0 copy-done.6
  90.7 0.1 multiply_reduce_fusion.1
  90.8 0.1 fusion.19
  91.0 18.6 %psum.15 = f32[4,8]{1,0:T(4,128)S(1)} all-reduce(f32[4,8]{1,0:T(4,128)S(1)} %bitcast.63), channel_id=1, replica_groups=mesh['run'=2,'tile'=4,'site'=2,'freq'=2] {'tile','site'}, use_global_device_ids=true, to_apply=%region_9.10 | all-reduce | flops 32 | bytes 256 | tf_op jit(solution)/shard_map/psum | solution.py:75
  109.5 0.6 broadcast_multiply_fusion.1
  110.1 0.0 copy-done.3
  (14 shorter events, 0.2 us)
Async XLA Ops:
  7.2 1.0 copy-start
  7.2 15.6 %copy-start.1 = (bf16[16,16,4,8,128]{4,3,2,1,0:T(8,128)(2,1)S(1)}, bf16[16,16,4,8,128]{4,3,2,1,0:T(8,128)(2,1)}, u32[]{:S(2)}) copy-start(bf16[16,16,4,8,128]{4,3,2,1,0:T(8,128)(2,1)} %param.7) | copy-start | bytes 6291460
  7.2 15.4 %copy-start.5 = (f32[16]{0:T(128)S(1)}, f32[16]{0:T(128)}, u32[]{:S(2)}) copy-start(f32[16]{0:T(128)} %param.11) | copy-start | bytes 196
  7.2 15.5 %copy-start.4 = (f32[16,4,8]{0,2,1:T(8,128)S(1)}, f32[16,4,8]{0,2,1:T(8,128)}, u32[]{:S(2)}) copy-start(f32[16,4,8]{0,2,1:T(8,128)} %param.10) | copy-start | bytes 6148
  13.0 13.6 %all-to-all-start = ((s32[8,1,64]{2,1,0:T(1,128)}), s32[8,1,64]{2,1,0:T(1,128)S(1)}, u32[]{:S(2)}, u32[]{:S(2)}) async-start(s32[8,1,64]{2,1,0:T(1,128)} %all_to_all.12), calls=%async_computation | async-start | bytes 8192 | tf_op jit(solution)/shard_map/all_to_all | solution.py:44
  23.4 44.7 %copy-start.2 = (f32[512,128]{1,0:T(8,128)S(1)}, f32[512,128]{1,0:T(8,128)}, u32[]{:S(2)}) copy-start(f32[512,128]{1,0:T(8,128)} %param.12) | copy-start | bytes 786436
  26.6 19.0 %all-to-all-start.1 = ((f32[8,64,256]{2,1,0:T(8,128)}), f32[8,64,256]{2,1,0:T(8,128)S(1)}, u32[]{:S(2)}, u32[]{:S(2)}) async-start(f32[8,64,256]{2,1,0:T(8,128)} %bitcast.11), calls=%async_computation.1 | async-start | bytes 1048576 | tf_op jit(solution)/shard_map/all_to_all | solution.py:37
  31.6 36.5 %all-reduce.3.cloned.1.call-start = ((), (), s32[]{:S(2)}) async-start(), calls=%async_computation.3 | async-start | bytes 1048576 | tf_op jit(solution)/shard_map/psum | solution.py:56
  71.8 13.2 %all-to-all-start.2 = ((bf16[8,64,128]{2,1,0:T(8,128)(2,1)}), bf16[8,64,128]{2,1,0:T(8,128)(2,1)S(1)}, u32[]{:S(2)}, u32[]{:S(2)}) async-start(bf16[8,64,128]{2,1,0:T(8,128)(2,1)} %bitcast.14), calls=%async_computation.2 | async-start | bytes 262144 | tf_op jit(solution)/shard_map/all_to_all | solution.py:62
  85.1 5.6 %copy-start.6 = (f32[8]{0:T(128)S(1)}, f32[8]{0:T(128)}, u32[]{:S(2)}) copy-start(f32[8]{0:T(128)} %param.13) | copy-start | bytes 100
  90.7 19.4 %copy-start.3 = (f32[16,1,4,8,1]{0,3,2,1,4:T(8,128)}, f32[16,1,4,8,1]{0,3,2,1,4:T(8,128)S(1)}, u32[]{:S(2)}) copy-start(f32[16,1,4,8,1]{0,3,2,1,4:T(8,128)S(1)} %copy.18) | copy-start | bytes 6148
Sparse Core Ops, SparseCore 0:
  50.3 17.8 all-reduce.2
where the time goes:
time: 117 us
  waiting for transfers between devices  39 us (33%)
  blocking collectives  18.6 us (16%)
  starting transfers between devices  18.1 us (15%)
  between operations  14.2 us (12%)
  local copies, waits for them, and re-layouts  11.6 us (10%)
  other arithmetic  10.1 us (9%)
  matrix products  5.41 us (5%)
    psum x1, blocking collectives, shards(): curve = lax.psum(partial_sum, ('tile', 'site')) / scale_total  18.6 us
    psum x1, waiting for transfers between devices, shards(): totals = lax.psum(totals, 'freq')  17.9 us
    all_to_all x1, waiting for transfers between devices, shards(): lax.all_to_all(outgoing.reshape(owner_count, capacity, 2 * width), ('tile...  12.7 us
    all_to_all x1, waiting for transfers between devices, shards(): lax.all_to_all(reply.reshape(owner_count, capacity, width), ('tile', 'sit...  7.43 us
    all_to_all x1, starting transfers between devices, shards(): lax.all_to_all(out_slots.reshape(owner_count, capacity), ('tile', 'site')...  7.25 us
    all_to_all x1, starting transfers between devices, shards(): lax.all_to_all(reply.reshape(owner_count, capacity, width), ('tile', 'sit...  5.78 us
    all_to_all x1, starting transfers between devices, shards(): lax.all_to_all(outgoing.reshape(owner_count, capacity, 2 * width), ('tile...  5 us
    dot_general x1, matrix products, shards(): jnp.einsum('skfcb,skb->sfc', jacobian, entry_step, preferred_element_type...  4.69 us
  transfers between devices with their start and end apart: 4, of which 4 were waited for; matrix products, arithmetic and copies ran while one was open for 6% of the time, Pallas kernels for 0%

commit v1 on v0

--- a/solution.py
+++ b/solution.py
@@ -72,7 +72,12 @@
     scale_total = site_count * owner_count * comps
     gap = residual[:, :, :, None] - step_lengths[None, None, None, :] * change[:, :, :, None]
     partial_sum = jnp.einsum("s,sfca->fa", weights, gap * gap)
-    curve = lax.psum(partial_sum, ("tile", "site")) / scale_total
+
+    def waves_advance(original):
+        value_now = lax.all_gather(original, axis_name=("tile", "site")).sum(axis=0)
+        return value_now
+
+    curve = waves_advance(partial_sum) / scale_total
     return (model_step, change, curve)
 
 

time: 117 us -> 125 us (1.068)
  blocking collectives: 18.6 us -> 26 us
    all_gather x0 -> x1, blocking collectives: none -> 26 us  [waves_advance(): value_now = lax.all_gather(original, axis_name=('tile', 'site')).sum(axis=0)]
    psum x1 -> x0, blocking collectives: 18.6 us -> none  [shards(): curve = lax.psum(partial_sum, ('tile', 'site')) / scale_total]
  transfers between devices with their start and end apart: 4 -> 4, of which waited for: 4 -> 4; matrix products, arithmetic and copies ran while one was open for 6% -> 5% of each run, Pallas kernels for 0% -> 0%
where the time goes in v1:
time: 125 us; the launch traced here: 124 us
  waiting for transfers between devices  39 us (31%)
  blocking collectives  26 us (21%)
  starting transfers between devices  18.1 us (14%)
  between operations  14.2 us (11%)
  local copies, waits for them, and re-layouts  11.6 us (9%)
  other arithmetic  10.1 us (8%)
  matrix products  5.41 us (4%)
    all_gather x1, blocking collectives, waves_advance(): value_now = lax.all_gather(original, axis_name=('tile', 'site')).sum(axis=0)  26 us
    psum x1, waiting for transfers between devices, shards(): totals = lax.psum(totals, 'freq')  17.9 us
    all_to_all x1, waiting for transfers between devices, shards(): lax.all_to_all(outgoing.reshape(owner_count, capacity, 2 * width), ('tile...  12.7 us
    all_to_all x1, waiting for transfers between devices, shards(): lax.all_to_all(reply.reshape(owner_count, capacity, width), ('tile', 'sit...  7.43 us
    all_to_all x1, starting transfers between devices, shards(): lax.all_to_all(out_slots.reshape(owner_count, capacity), ('tile', 'site')...  7.25 us
    all_to_all x1, starting transfers between devices, shards(): lax.all_to_all(reply.reshape(owner_count, capacity, width), ('tile', 'sit...  5.78 us
    all_to_all x1, starting transfers between devices, shards(): lax.all_to_all(outgoing.reshape(owner_count, capacity, 2 * width), ('tile...  5 us
    dot_general x1, matrix products, shards(): jnp.einsum('skfcb,skb->sfc', jacobian, entry_step, preferred_element_type...  4.69 us
  transfers between devices with their start and end apart: 4, of which 4 were waited for; matrix products, arithmetic and copies ran while one was open for 5% of the time, Pallas kernels for 0%

profile of v1, /device:TPU:0, one launch (start us, length us, event | category | flops | bytes accessed | tf_op | source)
XLA Modules:
  0.0 124.4 jit_solution(11161359256297389192)
XLA Ops:
  7.2 0.0 copy-start
  7.2 0.0 copy-start.1
  7.2 0.0 copy-start.5
  7.2 0.0 copy-start.4
  7.2 0.9 reshape.181
  8.2 0.0 copy-done
  8.2 1.7 %gather_fusion = s32[256]{0:T(256)S(1)} fusion(s32[4096]{0:T(1024)S(1)} %copy-done, s32[1024]{0:T(1024)S(1)} %pad_clamp_fusion.2), kind=kCustom, calls=%fused_computation | custom fusion | bytes 3072 | tf_op jit(solution)/shard_map/gather | solution.py:23
  9.9 0.6 reduce-window.6
  10.5 0.2 slice_reduce_fusion
  10.8 0.1 fusion.10
  10.9 1.4 %scatter_custom_fusion = s32[512]{0:T(512)S(1)} fusion(s32[256]{0:T(256)S(1)} %bitcast.65, s32[256]{0:T(256)S(1)} %get-tuple-element.5, s32[]{:T(128)} %constant.41.clone.1), kind=kCustom, calls=%fused_computation.49 | custom fusion | bytes 2052 | tf_op jit(solution)/shard_map/scatter | solution.py:34
  12.3 0.7 all_to_all.12
  13.0 7.3 %all-to-all-start = ((s32[8,1,64]{2,1,0:T(1,128)}), s32[8,1,64]{2,1,0:T(1,128)S(1)}, u32[]{:S(2)}, u32[]{:S(2)}) async-start(s32[8,1,64]{2,1,0:T(1,128)} %all_to_all.12), calls=%async_computation | async-start | bytes 8192 | tf_op jit(solution)/shard_map/all_to_all | solution.py:44
  20.2 2.3 %multiply_reduce_fusion = f32[16,16,128]{2,1,0:T(8,128)S(1)} fusion(bf16[16,16,4,8,128]{4,3,2,1,0:T(8,128)(2,1)} %param.7), kind=kLoop, calls=%fused_computation.6 | loop fusion | flops 3112960 | bytes 2228224 | tf_op jit(solution)/shard_map/reduce_sum | solution.py:19
  22.6 0.0 copy-done.5
  22.6 0.1 broadcast_multiply_fusion
  22.7 0.0 copy-done.4
  22.7 0.1 copy.16
  22.8 0.0 copy-done.1
  22.8 0.6 fusion.22
  23.4 0.0 copy-start.2
  23.4 2.2 %scatter_custom_fusion.1 = f32[512,256]{1,0:T(8,128)} fusion(s32[256]{0:T(256)S(1)} %bitcast.66, f32[256,256]{1,0:T(8,128)S(1)} %bitcast.57, f32[]{:T(128)} %constant.40.clone.1), kind=kCustom, calls=%fused_computation.14 | custom fusion | bytes 524292 | tf_op jit(solution)/shard_map/scatter | solution.py:32
  25.6 1.0 all-to-all-done
  26.6 5.0 %all-to-all-start.1 = ((f32[8,64,256]{2,1,0:T(8,128)}), f32[8,64,256]{2,1,0:T(8,128)S(1)}, u32[]{:S(2)}, u32[]{:S(2)}) async-start(f32[8,64,256]{2,1,0:T(8,128)} %bitcast.11), calls=%async_computation.1 | async-start | bytes 1048576 | tf_op jit(solution)/shard_map/all_to_all | solution.py:37
  31.6 0.0 all-reduce.3.cloned.1.call-start
  31.7 0.5 broadcast.204
  32.2 0.7 reduce.8
  32.8 0.1 reshape.231
  32.9 12.7 %all-to-all-done.1 = f32[8,64,256]{2,1,0:T(8,128)S(1)} async-done(((f32[8,64,256]{2,1,0:T(8,128)}), f32[8,64,256]{2,1,0:T(8,128)S(1)}, u32[]{:S(2)}, u32[]{:S(2)}) %all-to-all-start.1) | async-done | bytes 524320 | tf_op jit(solution)/shard_map/all_to_all | solution.py:37
  45.6 3.7 %scatter_custom_fusion.2 = f32[513,256]{1,0:T(8,128)S(1)} fusion(s32[512]{0:T(512)S(1)} %reshape.231, f32[512,256]{1,0:T(8,128)S(1)} %bitcast.55, f32[]{:T(128)} %constant.40.clone.1), kind=kCustom, calls=%fused_computation.9 | custom fusion | flops 131072 | bytes 525316 | tf_op jit(solution)/shard_map/scatter-add | solution.py:53
  49.3 0.8 slice.27
  50.1 0.0 all-reduce.3.cloned.1.call-update
  50.1 0.1 broadcast_in_dim_reshape.3
  50.2 17.9 %all-reduce.3.cloned.1.call-done = f32[512,256]{1,0:T(8,128)} async-done(((f32[512,256]{1,0:T(8,128)}), f32[512,256]{1,0:T(8,128)}) %all-reduce.3.cloned.1.call-update) | async-done | bytes 524304 | tf_op jit(solution)/shard_map/psum | solution.py:56
  68.1 0.0 copy-done.2
  68.1 1.8 %fusion.17 = (bf16[512,128]{1,0:T(8,128)(2,1)S(1)}, f32[512,128]{1,0:T(8,128)}) fusion(f32[512,128]{1,0:T(8,128)S(1)} %copy-done.2, f32[512,256]{1,0:T(8,128)} %all-reduce.3.cloned.1.call-done), kind=kLoop, calls=%fused_computation.55 | loop fusion | flops 196608 | bytes 1179648 | tf_op jit(solution)/shard_map/convert_element_type | solution.py:59
  69.9 1.9 %gather_fusion.1 = bf16[512,128]{1,0:T(8,128)(2,1)} fusion(bf16[513,128]{1,0:T(8,128)(2,1)S(1)} %concatenate.7, s32[1024]{0:T(1024)S(1)} %pad_clamp_fusion.1), kind=kCustom, calls=%fused_computation.1 | custom fusion | bytes 264192 | tf_op jit(solution)/shard_map/gather | solution.py:61
  71.8 5.8 %all-to-all-start.2 = ((bf16[8,64,128]{2,1,0:T(8,128)(2,1)}), bf16[8,64,128]{2,1,0:T(8,128)(2,1)S(1)}, u32[]{:S(2)}, u32[]{:S(2)}) async-start(bf16[8,64,128]{2,1,0:T(8,128)(2,1)} %bitcast.14), calls=%async_computation.2 | async-start | bytes 262144 | tf_op jit(solution)/shard_map/all_to_all | solution.py:62
  77.6 7.4 %all-to-all-done.2 = bf16[8,64,128]{2,1,0:T(8,128)(2,1)S(1)} async-done(((bf16[8,64,128]{2,1,0:T(8,128)(2,1)}), bf16[8,64,128]{2,1,0:T(8,128)(2,1)S(1)}, u32[]{:S(2)}, u32[]{:S(2)}) %all-to-all-start.2) | async-done | bytes 131104 | tf_op jit(solution)/shard_map/all_to_all | solution.py:62
  85.1 0.0 copy-start.6
  85.1 0.9 gather_fusion.2
  85.9 4.7 %fusion = f32[16,1,4,8,1]{3,1,4,2,0:T(1,128)S(1)} fusion(bf16[16,16,4,8,128]{4,3,2,1,0:T(8,128)(2,1)S(1)} %copy-done.1, bf16[16,16,128,1,1]{2,1,0,3,4:T(8,128)(2,1)S(1)} %bitcast.58), kind=kOutput, calls=%fused_computation.7 | convolution fusion | flops 2097152 | bytes 2164736 | tf_op jit(solution)/shard_map/skfcb,skb->sfc/dot_general | solution.py:71
  90.6 0.1 copy.20
  90.7 0.0 copy-start.3
  90.7 0.0 copy-done.6
  90.7 0.1 multiply_reduce_fusion.1
  90.8 0.1 fusion.19
  91.0 26.0 %all-gather.1 = f32[8,4,8]{2,1,0:T(4,128)S(1)} all-gather(f32[1,4,8]{2,1,0:T(4,128)S(1)} %bitcast.64), channel_id=2, replica_groups=mesh['run'=2,'tile'=4,'site'=2,'freq'=2] {'tile','site'}, dimensions={0}, use_global_device_ids=true | all-gather | bytes 1152 | tf_op jit(solution)/shard_map/all_gather | solution.py:77
  117.0 0.6 broadcast_multiply_fusion.1
  117.6 0.0 copy-done.3
  (15 shorter events, 0.2 us)
Async XLA Ops:
  7.2 1.0 copy-start
  7.2 15.6 %copy-start.1 = (bf16[16,16,4,8,128]{4,3,2,1,0:T(8,128)(2,1)S(1)}, bf16[16,16,4,8,128]{4,3,2,1,0:T(8,128)(2,1)}, u32[]{:S(2)}) copy-start(bf16[16,16,4,8,128]{4,3,2,1,0:T(8,128)(2,1)} %param.7) | copy-start | bytes 6291460
  7.2 15.4 %copy-start.5 = (f32[16]{0:T(128)S(1)}, f32[16]{0:T(128)}, u32[]{:S(2)}) copy-start(f32[16]{0:T(128)} %param.11) | copy-start | bytes 196
  7.2 15.5 %copy-start.4 = (f32[16,4,8]{0,2,1:T(8,128)S(1)}, f32[16,4,8]{0,2,1:T(8,128)}, u32[]{:S(2)}) copy-start(f32[16,4,8]{0,2,1:T(8,128)} %param.10) | copy-start | bytes 6148
  13.0 13.6 %all-to-all-start = ((s32[8,1,64]{2,1,0:T(1,128)}), s32[8,1,64]{2,1,0:T(1,128)S(1)}, u32[]{:S(2)}, u32[]{:S(2)}) async-start(s32[8,1,64]{2,1,0:T(1,128)} %all_to_all.12), calls=%async_computation | async-start | bytes 8192 | tf_op jit(solution)/shard_map/all_to_all | solution.py:44
  23.4 44.7 %copy-start.2 = (f32[512,128]{1,0:T(8,128)S(1)}, f32[512,128]{1,0:T(8,128)}, u32[]{:S(2)}) copy-start(f32[512,128]{1,0:T(8,128)} %param.12) | copy-start | bytes 786436
  26.6 19.0 %all-to-all-start.1 = ((f32[8,64,256]{2,1,0:T(8,128)}), f32[8,64,256]{2,1,0:T(8,128)S(1)}, u32[]{:S(2)}, u32[]{:S(2)}) async-start(f32[8,64,256]{2,1,0:T(8,128)} %bitcast.11), calls=%async_computation.1 | async-start | bytes 1048576 | tf_op jit(solution)/shard_map/all_to_all | solution.py:37
  31.6 36.5 %all-reduce.3.cloned.1.call-start = ((), (), s32[]{:S(2)}) async-start(), calls=%async_computation.3 | async-start | bytes 1048576 | tf_op jit(solution)/shard_map/psum | solution.py:56
  71.8 13.2 %all-to-all-start.2 = ((bf16[8,64,128]{2,1,0:T(8,128)(2,1)}), bf16[8,64,128]{2,1,0:T(8,128)(2,1)S(1)}, u32[]{:S(2)}, u32[]{:S(2)}) async-start(bf16[8,64,128]{2,1,0:T(8,128)(2,1)} %bitcast.14), calls=%async_computation.2 | async-start | bytes 262144 | tf_op jit(solution)/shard_map/all_to_all | solution.py:62
  85.1 5.6 %copy-start.6 = (f32[8]{0:T(128)S(1)}, f32[8]{0:T(128)}, u32[]{:S(2)}) copy-start(f32[8]{0:T(128)} %param.13) | copy-start | bytes 100
  90.7 26.9 %copy-start.3 = (f32[16,1,4,8,1]{0,3,2,1,4:T(8,128)}, f32[16,1,4,8,1]{0,3,2,1,4:T(8,128)S(1)}, u32[]{:S(2)}) copy-start(f32[16,1,4,8,1]{0,3,2,1,4:T(8,128)S(1)} %copy.20) | copy-start | bytes 6148
Sparse Core Ops, SparseCore 0:
  50.3 17.8 all-reduce.2
